TPU v7x, 32 devices: a whole 2x2x4 slice. The times are simulated.
32 devices in a mesh: band: 4 (over y, core), grid: 8 (over z, x).
Axes of the slice: x: 2, y: 2, z: 4, core: 2. Of those that a mesh axis runs over, the one named last changes fastest.
Arguments:
- bands: float32 [4, 2, 128, 128, 128], P('band', None, 'grid'), may hold values from -6 to 6
- coulomb: float32 [128, 128, 128], P(None, 'grid'), may hold values from 0.1 to 10
Outputs:
- exchange: float32 [4, 2, 128, 128, 128], P('band', None, 'grid')
All inputs are finite; a program needn't handle non-finite values.
Results may differ from a plain program's by a relative error of at most 0.0001.
Values sent between devices are 32-bit elements; how exact they have to be, the bound alone decides.
A program may use at most 64 MiB of HBM per device.

v0:
```python
import functools

import jax
import jax.numpy as jnp
import ml_dtypes
import numpy as np
from jax import lax
from jax.experimental import pallas as pl
from jax.experimental.pallas import tpu as pltpu
from jax.sharding import PartitionSpec as P

STEPS = 2
VMEM_LIMIT = 48 * 1024 * 1024


def split_table(table):
    high = table.astype(ml_dtypes.bfloat16)
    low = (table - high.astype(np.float64)).astype(ml_dtypes.bfloat16)
    return np.stack([high, low])


def tables(length, scale):
    index = np.arange(length)
    angle = (index[:, None] * index[None, :] % length) * (2.0 * np.pi / length)
    cosine, sine = np.cos(angle), np.sin(angle)
    forward = np.block([[cosine, sine], [-sine, cosine]])
    inverse = np.block([[cosine, -sine], [sine, cosine]])
    return [split_table(t) for t in (forward, inverse, inverse * scale, forward.T, inverse.T)]


def split(values):
    high = values.astype(jnp.bfloat16)
    return high, (values - high.astype(jnp.float32)).astype(jnp.bfloat16)


def dot(a, b):
    return jnp.dot(a, b, preferred_element_type=jnp.float32)


def left(table_ref, values):
    high, low = split(values)
    return dot(table_ref[0], high) + (dot(table_ref[1], high) + dot(table_ref[0], low))


def right(values, table_ref):
    high, low = split(values)
    return dot(high, table_ref[0]) + (dot(high, table_ref[1]) + dot(low, table_ref[0]))


def forward_kernel(own_ref, vis_ref, left_ref, right_ref, out_ref):
    planes, ny, nz = own_ref.shape[2:]
    shards, _, rows = out_ref.shape[:3]
    own_re, own_im, vis_re, vis_im = own_ref[0, 0], own_ref[0, 1], vis_ref[0, 0], vis_ref[0, 1]
    real = vis_re * own_re + vis_im * own_im
    imag = vis_re * own_im - vis_im * own_re
    pair = jnp.concatenate([real.reshape(planes * ny, nz), imag.reshape(planes * ny, nz)], axis=1)
    lines = right(pair, right_ref)
    for i in range(0, planes, 2):
        both = [
            jnp.concatenate([lines[p * ny:(p + 1) * ny, :nz], lines[p * ny:(p + 1) * ny, nz:]], axis=0)
            for p in (i, i + 1)
        ]
        result = left(left_ref, jnp.concatenate(both, axis=1))
        for p in range(2):
            for part in range(2):
                piece = result[part * ny:(part + 1) * ny, p * nz:(p + 1) * nz]
                out_ref[:, part, :, i + p, :] = piece.reshape(shards, rows, nz)


def pencil_kernel(in_ref, coulomb_ref, forward_ref, inverse_ref, out_ref):
    shards, _, rows, planes, nz = in_ref.shape
    nx = shards * planes
    for k in range(0, rows, 2):
        both = []
        for q in (k, k + 1):
            both.append(
                jnp.concatenate([in_ref[:, part, q].reshape(nx, nz) for part in range(2)], axis=0)
            )
        weight = jnp.concatenate([coulomb_ref[:, k, :], coulomb_ref[:, k + 1, :]], axis=1)
        value = left(forward_ref, jnp.concatenate(both, axis=1))
        value = value * jnp.concatenate([weight, weight], axis=0)
        value = left(inverse_ref, value)
        for q in range(2):
            for part in range(2):
                piece = value[part * nx:(part + 1) * nx, q * nz:(q + 1) * nz]
                out_ref[:, part, k + q] = piece.reshape(shards, planes, nz)


def inverse_kernel(has_base, in_ref, vis_ref, left_ref, right_ref, *rest):
    base_ref, out_ref = rest if has_base else (None, rest[0])
    shards, _, rows, planes, nz = in_ref.shape
    ny = shards * rows
    for i in range(0, planes, 2):
        both = []
        for p in (i, i + 1):
            both.append(
                jnp.concatenate([in_ref[:, part, :, p, :].reshape(ny, nz) for part in range(2)], axis=0)
            )
        result = left(left_ref, jnp.concatenate(both, axis=1))
        for p in range(2):
            cut = result[:, p * nz:(p + 1) * nz]
            value = right(jnp.concatenate([cut[:ny], cut[ny:]], axis=1), right_ref)
            pot_re, pot_im = -0.25 * value[:, :nz], -0.25 * value[:, nz:]
            vis_re, vis_im = vis_ref[0, 0, i + p], vis_ref[0, 1, i + p]
            out_re = pot_re * vis_re - pot_im * vis_im
            out_im = pot_re * vis_im + pot_im * vis_re
            if has_base:
                out_re = out_re + base_ref[0, 0, i + p]
                out_im = out_im + base_ref[0, 1, i + p]
            out_ref[0, 0, i + p] = out_re
            out_ref[0, 1, i + p] = out_im


def whole_spec(array):
    return pl.BlockSpec(array.shape, lambda i: (0,) * array.ndim)


def forward(own, vis, shards, tabs):
    _, _, planes, ny, nz = own.shape
    step = min(8, planes)
    slab = pl.BlockSpec((1, 2, step, ny, nz), lambda i: (0, 0, i, 0, 0))
    return pl.pallas_call(
        forward_kernel,
        grid=(planes // step,),
        in_specs=[slab, slab, whole_spec(tabs[0]), whole_spec(tabs[3])],
        out_specs=pl.BlockSpec((shards, 2, ny // shards, step, nz), lambda i: (0, 0, 0, i, 0)),
        out_shape=jax.ShapeDtypeStruct((shards, 2, ny // shards, planes, nz), jnp.float32),
        compiler_params=pltpu.CompilerParams(vmem_limit_bytes=VMEM_LIMIT),
        name="pair_density_dft",
    )(own, vis, tabs[0], tabs[3])


def pencil(block, coulomb, tabs):
    shards, _, rows, planes, nz = block.shape
    step = min(8, rows)
    spec = pl.BlockSpec((shards, 2, step, planes, nz), lambda i: (0, 0, i, 0, 0))
    return pl.pallas_call(
        pencil_kernel,
        grid=(rows // step,),
        in_specs=[
            spec,
            pl.BlockSpec((coulomb.shape[0], step, nz), lambda i: (0, i, 0)),
            whole_spec(tabs[0]),
            whole_spec(tabs[2]),
        ],
        out_specs=spec,
        out_shape=jax.ShapeDtypeStruct(block.shape, jnp.float32),
        compiler_params=pltpu.CompilerParams(vmem_limit_bytes=VMEM_LIMIT),
        name="screen_pencils",
    )(block, coulomb, tabs[0], tabs[2])


def inverse(block, vis, base, tabs):
    shards, _, rows, planes, nz = block.shape
    step = min(8, planes)
    slab = pl.BlockSpec((1, 2, step, shards * rows, nz), lambda i: (0, 0, i, 0, 0))
    extra = [] if base is None else [base]
    return pl.pallas_call(
        functools.partial(inverse_kernel, base is not None),
        grid=(planes // step,),
        in_specs=[
            pl.BlockSpec((shards, 2, rows, step, nz), lambda i: (0, 0, 0, i, 0)),
            slab,
            whole_spec(tabs[1]),
            whole_spec(tabs[4]),
        ] + [slab] * len(extra),
        out_specs=slab,
        out_shape=jax.ShapeDtypeStruct(vis.shape, jnp.float32),
        compiler_params=pltpu.CompilerParams(vmem_limit_bytes=VMEM_LIMIT),
        name="potential_to_exchange",
    )(block, vis, tabs[1], tabs[4], *extra)


def body(bands, coulomb):
    groups = lax.axis_size("band")
    shards = lax.axis_size("grid")
    span = groups // STEPS
    nx, ny, nz = coulomb.shape[0], bands.shape[3], bands.shape[4]
    tabs = [jnp.asarray(t) for t in tables(nx, 1.0 / (nx * ny * nz))]

    place = lax.axis_index("band") % span
    near = bands
    reach = 1
    while reach < span:
        moves = [(s * span + i, s * span + i + reach) for s in range(STEPS) for i in range(min(reach, span - reach))]
        arrived = lax.ppermute(near, "band", moves)
        near = jnp.where((place >= reach) & (place < 2 * reach), arrived, near)
        reach *= 2
    visitors = [near]
    for _ in range(STEPS - 1):
        visitors.append(lax.ppermute(visitors[-1], "band", [(i, (i + span) % groups) for i in range(groups)]))

    total = None
    sent = [forward(bands, vis, shards, tabs) for vis in visitors]
    sent = [lax.all_to_all(s, "grid", 0, 0, tiled=True) for s in sent]
    sent = [pencil(s, coulomb, tabs) for s in sent]
    sent = [lax.all_to_all(s, "grid", 0, 0, tiled=True) for s in sent]
    for block, vis in zip(sent, visitors):
        total = inverse(block, vis, total, tabs)
    return total


def solution(mesh):
    in_specs = (P("band", None, "grid", None, None), P(None, "grid", None))
    out_specs = P("band", None, "grid", None, None)
    return jax.shard_map(body, mesh=mesh, in_specs=in_specs, out_specs=out_specs, check_vma=False)
```

profile of v0, /device:TPU:28, one launch (start us, length us, event | category | flops | bytes accessed | tf_op | source)
XLA Modules:
  0.0 241.9 jit_solution(5080852901674641910)
XLA Ops:
  0.0 3.1 %collective-permute-start = (f32[1,2,16,128,128]{4,3,2,1,0:T(8,128)}, f32[1,2,16,128,128]{4,3,2,1,0:T(8,128)}, u32[]{:S(2)}, u32[]{:S(2)}) collective-permute-start(f32[1,2,16,128,128]{4,3,2,1,0:T(8,128)} %own_ref.3), channel_id=1, source_target_pairs={{0,8},{16,24},{1,9},{17,25},{2,10},{18,26},{3,11},{19,27},{4,12},{... | collective-permute-start | bytes 6291464 | tf_op jit(solution)/shard_map/ppermute | solution.py:186
  3.1 2.8 %collective-permute-done = f32[1,2,16,128,128]{4,3,2,1,0:T(8,128)} collective-permute-done((f32[1,2,16,128,128]{4,3,2,1,0:T(8,128)}, f32[1,2,16,128,128]{4,3,2,1,0:T(8,128)}, u32[]{:S(2)}, u32[]{:S(2)}) %collective-permute-start) | collective-permute-done | bytes 2097184 | tf_op jit(solution)/shard_map/ppermute | solution.py:186
  5.8 3.3 %broadcast_select_fusion.vis_ref = f32[1,2,16,128,128]{4,3,2,1,0:T(8,128)} fusion(f32[1,2,16,128,128]{4,3,2,1,0:T(8,128)} %collective-permute-done, f32[1,2,16,128,128]{4,3,2,1,0:T(8,128)} %own_ref.3, pred[]{:T(512)S(6)} %and.10), kind=kLoop, calls=%fused_computation | loop fusion | flops 524288 | bytes 6291457 | tf_op jit(solution)/shard_map/jit(_where)/select_n | solution.py:187
  9.1 5.3 %pair_density_dft.3 = f32[8,2,16,16,128]{4,3,2,1,0:T(8,128)S(1)} custom-call(f32[1,2,16,128,128]{4,3,2,1,0:T(8,128)S(1)} %copy-done, f32[1,2,16,128,128]{4,3,2,1,0:T(8,128)} %broadcast_select_fusion.vis_ref, bf16[2,256,256]{2,1,0:T(8,128)(2,1)S(1)} %copy-done.1, bf16[2,256,256]{2,1,0:T(8,128)(2,1)S(1)} %copy-done.14), custom_call_target="tpu_custom_call" | custom-call | tf_op jit(solution)/shard_map/pair_density_dft/pallas_call | solution.py:122
  14.4 1.3 copy-done.7
  15.8 6.0 %all-to-all-start.2 = ((f32[8,2,16,16,128]{4,3,2,1,0:T(8,128)}), f32[8,2,16,16,128]{4,3,2,1,0:T(8,128)}, u32[]{:S(2)}, u32[]{:S(2)}) async-start(f32[8,2,16,16,128]{4,3,2,1,0:T(8,128)} %copy-done.7), calls=%async_computation.2 | async-start | bytes 4194304 | tf_op jit(solution)/shard_map/all_to_all | solution.py:195
  22.3 47.0 %collective-permute-done.1.vis_ref = f32[1,2,16,128,128]{4,3,2,1,0:T(8,128)S(1)} collective-permute-done((f32[1,2,16,128,128]{4,3,2,1,0:T(8,128)}, f32[1,2,16,128,128]{4,3,2,1,0:T(8,128)S(1)}, u32[]{:S(2)}, u32[]{:S(2)}) %collective-permute-start.1) | collective-permute-done | bytes 2097184 | tf_op jit(solution)/shard_map/ppermute | solution.py:191
  70.7 5.3 %pair_density_dft.2 = f32[8,2,16,16,128]{4,3,2,1,0:T(8,128)S(1)} custom-call(f32[1,2,16,128,128]{4,3,2,1,0:T(8,128)S(1)} %copy-done, f32[1,2,16,128,128]{4,3,2,1,0:T(8,128)} %copy-done.2, bf16[2,256,256]{2,1,0:T(8,128)(2,1)S(1)} %copy-done.1, bf16[2,256,256]{2,1,0:T(8,128)(2,1)S(1)} %copy-done.14), custom_call_target="tpu_custom_call" | custom-call | tf_op jit(solution)/shard_map/pair_density_dft/pallas_call | solution.py:122
  76.0 1.4 copy-done.8
  77.4 6.1 %all-to-all-start = ((f32[8,2,16,16,128]{4,3,2,1,0:T(8,128)}), f32[8,2,16,16,128]{4,3,2,1,0:T(8,128)S(1)}, u32[]{:S(2)}, u32[]{:S(2)}) async-start(f32[8,2,16,16,128]{4,3,2,1,0:T(8,128)} %copy-done.8), calls=%async_computation | async-start | bytes 4194304 | tf_op jit(solution)/shard_map/all_to_all | solution.py:195
  84.5 4.0 %screen_pencils.3 = f32[8,2,16,16,128]{4,3,2,1,0:T(8,128)S(1)} custom-call(f32[8,2,16,16,128]{4,3,2,1,0:T(8,128)} %all-to-all-done.2.in_ref, f32[128,16,128]{2,1,0:T(8,128)S(1)} %copy-done.13, bf16[2,256,256]{2,1,0:T(8,128)(2,1)S(1)} %copy-done.1, bf16[2,256,256]{2,1,0:T(8,128)(2,1)S(1)} %copy-done.16), custom_call_target="tpu_custom_call" | custom-call | tf_op jit(solution)/shard_map/screen_pencils/pallas_call | solution.py:137
  88.5 1.3 copy-done.12
  89.8 39.0 %all-to-all-done.in_ref = f32[8,2,16,16,128]{4,3,2,1,0:T(8,128)S(1)} async-done(((f32[8,2,16,16,128]{4,3,2,1,0:T(8,128)}), f32[8,2,16,16,128]{4,3,2,1,0:T(8,128)S(1)}, u32[]{:S(2)}, u32[]{:S(2)}) %all-to-all-start) | async-done | bytes 2097184 | tf_op jit(solution)/shard_map/all_to_all | solution.py:195
  130.1 5.8 %all-to-all-start.3 = ((f32[8,2,16,16,128]{4,3,2,1,0:T(8,128)}), f32[8,2,16,16,128]{4,3,2,1,0:T(8,128)S(1)}, u32[]{:S(2)}, u32[]{:S(2)}) async-start(f32[8,2,16,16,128]{4,3,2,1,0:T(8,128)} %copy-done.12), calls=%async_computation.3 | async-start | bytes 4194304 | tf_op jit(solution)/shard_map/all_to_all | solution.py:197
  135.9 1.6 copy-done.10
  138.5 3.0 %screen_pencils.2 = f32[8,2,16,16,128]{4,3,2,1,0:T(8,128)S(1)} custom-call(f32[8,2,16,16,128]{4,3,2,1,0:T(8,128)S(1)} %copy-done.10, f32[128,16,128]{2,1,0:T(8,128)S(1)} %copy-done.13, bf16[2,256,256]{2,1,0:T(8,128)(2,1)S(1)} %copy-done.1, bf16[2,256,256]{2,1,0:T(8,128)(2,1)S(1)} %copy-done.17), custom_call_target="tpu_custom_call" | custom-call | tf_op jit(solution)/shard_map/screen_pencils/pallas_call | solution.py:137
  142.7 40.1 %all-to-all-done.3.in_ref = f32[8,2,16,16,128]{4,3,2,1,0:T(8,128)S(1)} async-done(((f32[8,2,16,16,128]{4,3,2,1,0:T(8,128)}), f32[8,2,16,16,128]{4,3,2,1,0:T(8,128)S(1)}, u32[]{:S(2)}, u32[]{:S(2)}) %all-to-all-start.3) | async-done | bytes 2097184 | tf_op jit(solution)/shard_map/all_to_all | solution.py:197
  182.8 1.4 copy-done.5
  184.2 5.8 %all-to-all-start.1 = ((f32[8,2,16,16,128]{4,3,2,1,0:T(8,128)}), f32[8,2,16,16,128]{4,3,2,1,0:T(8,128)}, u32[]{:S(2)}, u32[]{:S(2)}) async-start(f32[8,2,16,16,128]{4,3,2,1,0:T(8,128)} %copy-done.11), calls=%async_computation.1 | async-start | bytes 4194304 | tf_op jit(solution)/shard_map/all_to_all | solution.py:197
  190.0 1.6 copy-done.6
  191.6 4.7 %potential_to_exchange.2.rest_0_ = f32[1,2,16,128,128]{4,3,2,1,0:T(8,128)S(1)} custom-call(f32[8,2,16,16,128]{4,3,2,1,0:T(8,128)S(1)} %copy-done.6, f32[1,2,16,128,128]{4,3,2,1,0:T(8,128)} %broadcast_select_fusion.vis_ref, bf16[2,256,256]{2,1,0:T(8,128)(2,1)S(1)} %copy-done.15, bf16[2,256,256]{2,1,0:T(8,128)(2,1)S(1)} %copy-done.1), custom_call_target="tpu_custom_call" | custom-call | tf_op jit(solution)/shard_map/potential_to_exchange/pallas_call | solution.py:158
  196.3 1.4 copy-done.4
  197.7 38.5 %all-to-all-done.1.in_ref = f32[8,2,16,16,128]{4,3,2,1,0:T(8,128)} async-done(((f32[8,2,16,16,128]{4,3,2,1,0:T(8,128)}), f32[8,2,16,16,128]{4,3,2,1,0:T(8,128)}, u32[]{:S(2)}, u32[]{:S(2)}) %all-to-all-start.1) | async-done | bytes 2097184 | tf_op jit(solution)/shard_map/all_to_all | solution.py:197
  236.2 5.7 %potential_to_exchange.3 = f32[1,2,16,128,128]{4,3,2,1,0:T(8,128)} custom-call(f32[8,2,16,16,128]{4,3,2,1,0:T(8,128)} %all-to-all-done.1.in_ref, f32[1,2,16,128,128]{4,3,2,1,0:T(8,128)S(1)} %copy-done.3, bf16[2,256,256]{2,1,0:T(8,128)(2,1)S(1)} %copy-done.15, bf16[2,256,256]{2,1,0:T(8,128)(2,1)S(1)} %copy-done.1, f32[1,2,16,128,128]{4,3,2,1,0:T(8,128)} %copy-done.4), custom_call_target="tpu_custom_call" | custom-call | tf_op jit(solution)/shard_map/potential_to_exchange/pallas_call | solution.py:158
  (31 shorter events, 6.4 us)
Async XLA Ops:
  0.0 5.8 %collective-permute-start = (f32[1,2,16,128,128]{4,3,2,1,0:T(8,128)}, f32[1,2,16,128,128]{4,3,2,1,0:T(8,128)}, u32[]{:S(2)}, u32[]{:S(2)}) collective-permute-start(f32[1,2,16,128,128]{4,3,2,1,0:T(8,128)} %own_ref.3), channel_id=1, source_target_pairs={{0,8},{16,24},{1,9},{17,25},{2,10},{18,26},{3,11},{19,27},{4,12},{... | collective-permute-start | bytes 6291464 | tf_op jit(solution)/shard_map/ppermute | solution.py:186
  3.1 6.0 %copy-start = (f32[1,2,16,128,128]{4,3,2,1,0:T(8,128)S(1)}, f32[1,2,16,128,128]{4,3,2,1,0:T(8,128)}, u32[]{:S(2)}) copy-start(f32[1,2,16,128,128]{4,3,2,1,0:T(8,128)} %own_ref.3) | copy-start | bytes 6291460
  3.1 6.0 %copy-start.1 = (bf16[2,256,256]{2,1,0:T(8,128)(2,1)S(1)}, bf16[2,256,256]{2,1,0:T(8,128)(2,1)}, u32[]{:S(2)}) copy-start(bf16[2,256,256]{2,1,0:T(8,128)(2,1)} %constant.25.clone.left_ref.forward_ref.right_ref) | copy-start | bytes 786436
  3.1 6.0 %copy-start.14 = (bf16[2,256,256]{2,1,0:T(8,128)(2,1)S(1)}, bf16[2,256,256]{2,1,0:T(8,128)(2,1)}, u32[]{:S(2)}) copy-start(bf16[2,256,256]{2,1,0:T(8,128)(2,1)} %constant.26.clone.right_ref.left_ref) | copy-start | bytes 786436
  14.4 1.4 copy-start.7
  15.8 61.6 %all-to-all-start.2 = ((f32[8,2,16,16,128]{4,3,2,1,0:T(8,128)}), f32[8,2,16,16,128]{4,3,2,1,0:T(8,128)}, u32[]{:S(2)}, u32[]{:S(2)}) async-start(f32[8,2,16,16,128]{4,3,2,1,0:T(8,128)} %copy-done.7), calls=%async_computation.2 | async-start | bytes 4194304 | tf_op jit(solution)/shard_map/all_to_all | solution.py:195
  21.8 47.5 %collective-permute-start.1 = (f32[1,2,16,128,128]{4,3,2,1,0:T(8,128)}, f32[1,2,16,128,128]{4,3,2,1,0:T(8,128)S(1)}, u32[]{:S(2)}, u32[]{:S(2)}) collective-permute-start(f32[1,2,16,128,128]{4,3,2,1,0:T(8,128)} %broadcast_select_fusion.vis_ref), channel_id=1, source_target_pairs={{0,16},{8,24},{16,0},{24,8},{1,17},{9,25},{17,1},{25,9},{2,18},{10... | collective-permute-start | bytes 6291464 | tf_op jit(solution)/shard_map/ppermute | solution.py:191
  69.4 1.3 copy-start.2
  76.0 1.4 copy-start.8
  77.4 6.1 %copy-start.13 = (f32[128,16,128]{2,1,0:T(8,128)S(1)}, f32[128,16,128]{2,1,0:T(8,128)}, u32[]{:S(2)}) copy-start(f32[128,16,128]{2,1,0:T(8,128)} %coulomb_ref.3) | copy-start | bytes 3145732
  77.4 51.4 %all-to-all-start = ((f32[8,2,16,16,128]{4,3,2,1,0:T(8,128)}), f32[8,2,16,16,128]{4,3,2,1,0:T(8,128)S(1)}, u32[]{:S(2)}, u32[]{:S(2)}) async-start(f32[8,2,16,16,128]{4,3,2,1,0:T(8,128)} %copy-done.8), calls=%async_computation | async-start | bytes 4194304 | tf_op jit(solution)/shard_map/all_to_all | solution.py:195
  83.6 1.0 copy-start.16
  88.5 1.4 copy-start.12
  128.8 1.3 copy-start.9
  130.1 52.6 %all-to-all-start.3 = ((f32[8,2,16,16,128]{4,3,2,1,0:T(8,128)}), f32[8,2,16,16,128]{4,3,2,1,0:T(8,128)S(1)}, u32[]{:S(2)}, u32[]{:S(2)}) async-start(f32[8,2,16,16,128]{4,3,2,1,0:T(8,128)} %copy-done.12), calls=%async_computation.3 | async-start | bytes 4194304 | tf_op jit(solution)/shard_map/all_to_all | solution.py:197
  135.9 1.6 copy-start.10
  137.5 0.9 copy-start.17
  141.4 1.3 copy-start.11
  142.7 47.3 %copy-start.15 = (bf16[2,256,256]{2,1,0:T(8,128)(2,1)S(1)}, bf16[2,256,256]{2,1,0:T(8,128)(2,1)}, u32[]{:S(2)}) copy-start(bf16[2,256,256]{2,1,0:T(8,128)(2,1)} %constant.26.clone.right_ref.left_ref) | copy-start | bytes 786436
  182.8 1.4 copy-start.5
  184.2 52.0 %all-to-all-start.1 = ((f32[8,2,16,16,128]{4,3,2,1,0:T(8,128)}), f32[8,2,16,16,128]{4,3,2,1,0:T(8,128)}, u32[]{:S(2)}, u32[]{:S(2)}) async-start(f32[8,2,16,16,128]{4,3,2,1,0:T(8,128)} %copy-done.11), calls=%async_computation.1 | async-start | bytes 4194304 | tf_op jit(solution)/shard_map/all_to_all | solution.py:197
  190.0 1.6 copy-start.6
  191.6 44.6 %copy-start.3 = (f32[1,2,16,128,128]{4,3,2,1,0:T(8,128)S(1)}, f32[1,2,16,128,128]{4,3,2,1,0:T(8,128)}, u32[]{:S(2)}) copy-start(f32[1,2,16,128,128]{4,3,2,1,0:T(8,128)} %copy-done.2) | copy-start | bytes 6291460
  196.3 1.4 copy-start.4
where the time goes:
time: 245 us; the launch traced here: 242 us
  waiting for transfers between devices  167 us (68%)
  Pallas kernels  27.9 us (11%)
  starting transfers between devices  27.3 us (11%)
  local copies, waits for them, and re-layouts  15.9 us (6%)
  other arithmetic  3.26 us (1%)
    all_to_all x4, waiting for transfers between devices, body(): sent = [lax.all_to_all(s, 'grid', 0, 0, tiled=True) for s in sent]  118 us
    ppermute x1, waiting for transfers between devices, body(): lax.ppermute(visitors[-1], 'band', [(i, (i + span) % groups) for i in ran...  47 us
    all_to_all x4, starting transfers between devices, body(): sent = [lax.all_to_all(s, 'grid', 0, 0, tiled=True) for s in sent]  23.8 us
    unnamed x36, local copies, waits for them, and re-layouts  15.9 us
    pallas_call x2, Pallas kernels, forward(): pl.pallas_call(forward_kernel, grid=(planes // step,), in_specs=[slab, sl...  10.6 us
    pallas_call x2, Pallas kernels, inverse(): pl.pallas_call(functools.partial(inverse_kernel, base is not None), grid=...  10.4 us
    pallas_call x2, Pallas kernels, pencil(): pl.pallas_call(pencil_kernel, grid=(rows // step,), in_specs=[spec, pl.Bl...  6.94 us
  transfers between devices with their start and end apart: 6, of which 5 were waited for; matrix products, arithmetic and copies ran while one was open for 0% of the time, Pallas kernels for 7%

commit v1 on v0

--- a/solution.py
+++ b/solution.py
@@ -171,7 +171,7 @@
     )(block, vis, tabs[1], tabs[4], *extra)
 
 
-def body(bands, coulomb):
+def by_pairs(bands, coulomb):
     groups = lax.axis_size("band")
     shards = lax.axis_size("grid")
     span = groups // STEPS
@@ -200,6 +200,436 @@
     return total
 
 
+def permuted_tables(length, scale, row_order, plane_order):
+    index = np.arange(length)
+    angle = (index[:, None] * index[None, :] % length) * (2.0 * np.pi / length)
+    cosine, sine = np.cos(angle), np.sin(angle)
+    forward = np.block([[cosine, sine], [-sine, cosine]])
+    inverse = np.block([[cosine, -sine], [sine, cosine]])
+    rows = np.concatenate([row_order, row_order + length])
+    planes = np.concatenate([plane_order, plane_order + length])
+    return [
+        split_table(t)
+        for t in (
+            forward.T,
+            forward[rows],
+            forward[:, planes],
+            inverse[planes] * scale,
+            inverse[:, rows],
+            inverse.T,
+        )
+    ]
+
+
+GROUPS = 4
+HALVES = 2
+PLANE_BAND = (0, 1, 3, 2)
+PLANE_SLOT = (0, 2, 3, 1)
+
+
+def fused_kernel(
+    spread,
+    bands_ref, coulomb_ref, zf_ref, yf_ref, xf_ref, xi_ref, yi_ref, zi_ref,
+    out_ref,
+    held, screen, packed, lines, back, result, slab,
+    s1, r1, s2, r2, su, ru, sd, rd, s4, r4, s6, r6, s7, r7, s8, r8, loc,
+):
+    n = GROUPS
+    peers = n * spread
+    band = lax.axis_index("band")
+    grid = lax.axis_index("grid")
+    z = grid // spread
+    t = grid % spread
+    me = band * spread + t
+    ny, nz = bands_ref.shape[3], bands_ref.shape[4]
+    rows = ny // peers
+    nx = peers * 2 * n * HALVES
+
+    def remote(src, dst, send, recv, to_band, to_grid):
+        return pltpu.make_async_remote_copy(
+            src_ref=src, dst_ref=dst, send_sem=send, recv_sem=recv,
+            device_id=(to_band, to_grid), device_id_type=pl.DeviceIdType.MESH,
+        )
+
+    def peer(k):
+        q = (me + k) % peers
+        return q, q // spread, z * spread + q % spread
+
+    def line(k):
+        return k * spread + t
+
+    barrier = pltpu.get_barrier_semaphore()
+    for k in range(1, peers):
+        _, to_band, to_grid = peer(k)
+        pl.semaphore_signal(barrier, inc=1, device_id=(to_band, to_grid), device_id_type=pl.DeviceIdType.MESH)
+    for k in range(1, n):
+        pl.semaphore_signal(
+            barrier, inc=1, device_id=(band, line((z + k) % n)), device_id_type=pl.DeviceIdType.MESH
+        )
+    pl.semaphore_wait(barrier, peers - 1 + n - 1)
+
+    slot = (band % 2) * 2 + band // 2
+
+    def chunk(h, j):
+        return bands_ref.at[0, :, pl.ds(j * n + h * 2, 2)]
+
+    def first(h, d):
+        to = (band + d) % n
+        return remote(chunk(h, to), held.at[h, z, slot], s1.at[h, d], r1.at[h, d], to, grid)
+
+    def first_local(h):
+        return pltpu.make_async_copy(chunk(h, band), held.at[h, z, slot], loc.at[h])
+
+    screen_local = pltpu.make_async_copy(coulomb_ref, screen.at[z], loc.at[HALVES])
+    screen_local.start()
+    for h in range(HALVES):
+        first_local(h).start()
+        for d in (2, 1, 3):
+            first(h, d).start()
+
+    def block(stream, src):
+        return held.at[stream, src, pl.ds(0, 2)] if stream < HALVES else screen.at[src]
+
+    def up(stream, d):
+        return remote(
+            block(stream, z - d), block(stream, z - d), su.at[stream, d], ru.at[stream, d], band, line(z + 1)
+        )
+
+    def down(stream, d):
+        return remote(
+            block(stream, z + d), block(stream, z + d), sd.at[stream, d], rd.at[stream, d], band, line(z - 1)
+        )
+
+    def hop(stream, d):
+        if d > 0:
+            @pl.when(z >= d)
+            def _():
+                pltpu.make_async_remote_copy(
+                    src_ref=block(stream, z - d), dst_ref=block(stream, z - d),
+                    send_sem=su.at[stream, d], recv_sem=ru.at[stream, d - 1],
+                    device_id=(band, grid), device_id_type=pl.DeviceIdType.MESH,
+                ).wait_recv()
+
+            @pl.when(z + d < n)
+            def _():
+                pltpu.make_async_remote_copy(
+                    src_ref=block(stream, z + d), dst_ref=block(stream, z + d),
+                    send_sem=sd.at[stream, d], recv_sem=rd.at[stream, d - 1],
+                    device_id=(band, grid), device_id_type=pl.DeviceIdType.MESH,
+                ).wait_recv()
+        if d < n - 1:
+            @pl.when((z >= d) & (z + 1 < n))
+            def _():
+                up(stream, d).start()
+
+            @pl.when((z + d < n) & (z >= 1))
+            def _():
+                down(stream, d).start()
+
+    def hops_sent(stream):
+        for d in range(n - 1):
+            @pl.when((z >= d) & (z + 1 < n))
+            def _():
+                up(stream, d).wait_send()
+
+            @pl.when((z + d < n) & (z >= 1))
+            def _():
+                down(stream, d).wait_send()
+
+    def direct(h, c):
+        to = c + 1
+        part = held.at[h, z, 2 + c]
+        return remote(part, part, s2.at[h, c], r2.at[h, z], band, line(to))
+
+    for h in range(HALVES):
+        first_local(h).wait()
+        for d in range(1, n):
+            first(h, d).wait_recv()
+        hop(h, 0)
+        for c in range(2):
+            @pl.when(z != c + 1)
+            def _():
+                direct(h, c).start()
+        if h == 0:
+            hop(0, 1)
+    screen_local.wait()
+    hop(1, 1)
+    hop(0, 2)
+    hop(HALVES, 0)
+
+    own = jnp.where(z == 0, 0, jnp.where(z == 1, 2, jnp.where(z == 2, 3, 1)))
+
+    def received(h):
+        for src in range(n):
+            @pl.when((z != src) & ((z == 1) | (z == 2)))
+            def _():
+                part = held.at[h, src, 2]
+                pltpu.make_async_remote_copy(
+                    src_ref=part, dst_ref=held.at[h, src, own],
+                    send_sem=s2.at[h, 0], recv_sem=r2.at[h, src],
+                    device_id=(band, grid), device_id_type=pl.DeviceIdType.MESH,
+                ).wait_recv()
+
+    def fourth(h, k):
+        q, to_band, to_grid = peer(k)
+        return remote(packed.at[h, q], lines.at[h, me], s4.at[h, k], r4.at[h, k], to_band, to_grid)
+
+    def fourth_local(h):
+        return pltpu.make_async_copy(packed.at[h, me], lines.at[h, me], loc.at[3 + h])
+
+    def densities(h):
+        @pl.loop(0, 2)
+        def _(v):
+            reals, imags = [], []
+            for src in range(n):
+                for p in range(2):
+                    own_re, own_im = held[h, src, own, 0, p], held[h, src, own, 1, p]
+                    vis_re, vis_im = held[h, src, v, 0, p], held[h, src, v, 1, p]
+                    reals.append(vis_re * own_re + vis_im * own_im)
+                    imags.append(vis_re * own_im - vis_im * own_re)
+            pair = jnp.concatenate([jnp.concatenate(reals, axis=0), jnp.concatenate(imags, axis=0)], axis=1)
+            value = right(pair, zf_ref)
+            for i in range(0, 2 * n, 2):
+                both = [
+                    jnp.concatenate([value[p * ny:(p + 1) * ny, :nz], value[p * ny:(p + 1) * ny, nz:]], axis=0)
+                    for p in (i, i + 1)
+                ]
+                done = left(yf_ref, jnp.concatenate(both, axis=1))
+                for p in range(2):
+                    for part in range(2):
+                        piece = done[part * ny:(part + 1) * ny, p * nz:(p + 1) * nz]
+                        packed[h, :, v, :, part, i + p, :] = piece.reshape(peers, rows, nz)
+
+    for h in range(HALVES):
+        hop(h, 3)
+        received(h)
+        densities(h)
+        fourth_local(h).start()
+        for k in range(1, peers):
+            fourth(h, k).start()
+        if h == 0:
+            hop(HALVES, 1)
+            hop(1, 2)
+            hop(HALVES, 2)
+    hop(HALVES, 3)
+
+    for h in range(HALVES):
+        fourth_local(h).wait()
+        for k in range(1, peers):
+            fourth(h, k).wait()
+
+    @pl.loop(0, n)
+    def _(src):
+        for v in range(2):
+            for c in range(0, n, 2):
+                both = [
+                    jnp.concatenate(
+                        [lines[:, :, v, src * n + c + p, part].reshape(nx, nz) for part in range(2)], axis=0
+                    )
+                    for p in range(2)
+                ]
+                weight = jnp.concatenate([screen[src, c], screen[src, c + 1]], axis=1)
+                value = left(xf_ref, jnp.concatenate(both, axis=1))
+                value = value * jnp.concatenate([weight, weight], axis=0)
+                value = left(xi_ref, value)
+                for p in range(2):
+                    for part in range(2):
+                        piece = value[part * nx:(part + 1) * nx, p * nz:(p + 1) * nz]
+                        packed[:, :, v, src * n + c + p, part] = piece.reshape(HALVES, peers, 2 * n, nz)
+
+    def sixth(h, k):
+        q, to_band, to_grid = peer(k)
+        return remote(packed.at[h, q], back.at[h, me], s6.at[h, k], r6.at[h, k], to_band, to_grid)
+
+    def sixth_local(h):
+        return pltpu.make_async_copy(packed.at[h, me], back.at[h, me], loc.at[5 + h])
+
+    def seventh(h, to):
+        return remote(result.at[h, to], slab.at[h, z], s7.at[h, to], r7.at[h, z], band, line(to))
+
+    def seventh_local(h, to):
+        return pltpu.make_async_copy(result.at[h, to], slab.at[h, to], loc.at[7 + h])
+
+    def out_part(j, h):
+        return out_ref.at[0, :, pl.ds(j * n + h * 2, 2)]
+
+    def eighth(h, src):
+        return remote(slab.at[h, src], out_part(band, h), s8.at[h, src], r8.at[h, band], PLANE_BAND[src], grid)
+
+    def eighth_local(h, src):
+        return pltpu.make_async_copy(slab.at[h, src], out_part(band, h), loc.at[9 + h])
+
+    for h in range(HALVES):
+        sixth_local(h).start()
+        for k in range(1, peers):
+            sixth(h, k).start()
+
+    def deliver(h):
+        for src in range(n):
+            @pl.when(z == src)
+            def _():
+                seventh_local(h, src).wait()
+
+            @pl.when(z != src)
+            def _():
+                pltpu.make_async_remote_copy(
+                    src_ref=result.at[h, src], dst_ref=slab.at[h, src],
+                    send_sem=s7.at[h, src], recv_sem=r7.at[h, src],
+                    device_id=(band, grid), device_id_type=pl.DeviceIdType.MESH,
+                ).wait_recv()
+
+            @pl.when(band == PLANE_BAND[src])
+            def _():
+                eighth_local(h, src).start()
+
+            @pl.when(band != PLANE_BAND[src])
+            def _():
+                eighth(h, src).start()
+
+    for h in range(HALVES):
+        sixth_local(h).wait()
+        for k in range(1, peers):
+            sixth(h, k).wait_recv()
+        for src in range(n):
+            for p in range(2):
+                i = src * 2 + p
+                both = [
+                    jnp.concatenate([back[h, :, v, :, part, i, :].reshape(ny, nz) for part in range(2)], axis=0)
+                    for v in range(2)
+                ]
+                value = left(yi_ref, jnp.concatenate(both, axis=1))
+                value = jnp.concatenate(
+                    [
+                        jnp.concatenate([value[:ny, v * nz:(v + 1) * nz], value[ny:, v * nz:(v + 1) * nz]], axis=1)
+                        for v in range(2)
+                    ],
+                    axis=0,
+                )
+                value = -0.25 * right(value, zi_ref)
+                total_re, total_im = 0.0, 0.0
+                for v in range(2):
+                    pot_re, pot_im = value[v * ny:(v + 1) * ny, :nz], value[v * ny:(v + 1) * ny, nz:]
+                    vis_re, vis_im = held[h, src, v, 0, p], held[h, src, v, 1, p]
+                    total_re = total_re + (pot_re * vis_re - pot_im * vis_im)
+                    total_im = total_im + (pot_re * vis_im + pot_im * vis_re)
+                result[h, src, 0, p] = total_re
+                result[h, src, 1, p] = total_im
+
+            @pl.when(z == src)
+            def _():
+                seventh_local(h, src).start()
+
+            @pl.when(z != src)
+            def _():
+                seventh(h, src).start()
+    for h in range(HALVES):
+        deliver(h)
+
+    for h in range(HALVES):
+        for d in range(1, n):
+            first(h, d).wait_send()
+        for c in range(2):
+            @pl.when(z != c + 1)
+            def _():
+                direct(h, c).wait_send()
+        for k in range(1, peers):
+            sixth(h, k).wait_send()
+        for src in range(n):
+            @pl.when(z != src)
+            def _():
+                seventh(h, src).wait_send()
+
+            @pl.when(band == PLANE_BAND[src])
+            def _():
+                eighth_local(h, src).wait()
+
+            @pl.when(band != PLANE_BAND[src])
+            def _():
+                eighth(h, src).wait_send()
+
+            @pl.when(band != src)
+            def _():
+                pltpu.make_async_remote_copy(
+                    src_ref=slab.at[h, 0], dst_ref=out_part(src, h),
+                    send_sem=s8.at[h, src], recv_sem=r8.at[h, src],
+                    device_id=(band, grid), device_id_type=pl.DeviceIdType.MESH,
+                ).wait_recv()
+    for stream in range(HALVES + 1):
+        hops_sent(stream)
+
+
+def fused(bands, coulomb):
+    n = GROUPS
+    spread = lax.axis_size("grid") // n
+    peers = n * spread
+    nx, ny, nz = coulomb.shape[0], bands.shape[3], bands.shape[4]
+    rows = ny // peers
+    q = np.arange(peers)
+    row_order = (
+        (np.arange(n)[None, :, None] * spread + (q % spread)[:, None, None]) * rows
+        + (q // spread)[:, None, None] * n
+        + np.arange(n)[None, None, :]
+    ).reshape(-1)
+    plane_order = (
+        np.arange(n)[None, None, :, None] * (nx // n)
+        + (q % spread)[None, :, None, None] * (nx // n // spread)
+        + (q // spread)[None, :, None, None] * n
+        + np.arange(HALVES)[:, None, None, None] * 2
+        + np.arange(2)
+    ).reshape(-1)
+    tabs = [jnp.asarray(t) for t in permuted_tables(nx, 1.0 / (nx * ny * nz), row_order, plane_order)]
+    mine = lax.dynamic_slice_in_dim(coulomb, lax.axis_index("band") * n, n, axis=1).transpose(1, 0, 2)
+    f32 = jnp.float32
+    blocks = (HALVES, peers, 2, rows, 2, 2 * n, nz)
+    sem = pltpu.SemaphoreType.DMA
+    return pl.pallas_call(
+        functools.partial(fused_kernel, spread),
+        in_specs=[pl.BlockSpec(memory_space=pl.ANY)] * 2 + [pl.BlockSpec(memory_space=pltpu.VMEM)] * 6,
+        out_specs=pl.BlockSpec(memory_space=pl.ANY),
+        out_shape=jax.ShapeDtypeStruct(bands.shape, f32),
+        scratch_shapes=[
+            pltpu.VMEM((HALVES, n, n, 2, 2, ny, nz), f32),
+            pltpu.VMEM((n, n, nx, nz), f32),
+            pltpu.VMEM(blocks, f32),
+            pltpu.VMEM(blocks, f32),
+            pltpu.VMEM(blocks, f32),
+            pltpu.VMEM((HALVES, n, 2, 2, ny, nz), f32),
+            pltpu.VMEM((HALVES, n, 2, 2, ny, nz), f32),
+            sem((HALVES, n)), sem((HALVES, n)),
+            sem((HALVES, 2)), sem((HALVES, n)),
+            sem((HALVES + 1, n)), sem((HALVES + 1, n)),
+            sem((HALVES + 1, n)), sem((HALVES + 1, n)),
+            sem((HALVES, peers)), sem((HALVES, peers)),
+            sem((HALVES, peers)), sem((HALVES, peers)),
+            sem((HALVES, n)), sem((HALVES, n)),
+            sem((HALVES, n)), sem((HALVES, n)),
+            sem((11,)),
+        ],
+        compiler_params=pltpu.CompilerParams(
+            collective_id=0, has_side_effects=True, vmem_limit_bytes=VMEM_LIMIT
+        ),
+        name="exchange_by_planes",
+    )(bands, mine, *tabs)
+
+
+def fits(bands, coulomb):
+    groups, shards = lax.axis_size("band"), lax.axis_size("grid")
+    return (
+        bands.shape[0] == 1
+        and groups == GROUPS
+        and shards % GROUPS == 0
+        and bands.shape[2] == 2 * HALVES * GROUPS
+        and bands.shape[3] == GROUPS * GROUPS * shards
+        and coulomb.shape[0] == bands.shape[3] == bands.shape[4]
+    )
+
+
+def body(bands, coulomb):
+    if fits(bands, coulomb):
+        return fused(bands, coulomb)
+    return by_pairs(bands, coulomb)
+
+
 def solution(mesh):
     in_specs = (P("band", None, "grid", None, None), P(None, "grid", None))
     out_specs = P("band", None, "grid", None, None)

time: 245 us -> 241 us (0.984); the launches traced: 242 us -> 241 us
  Pallas kernels: 27.9 us -> 231 us
  waiting for transfers between devices: 167 us -> 0 us
  starting transfers between devices: 27.3 us -> 0 us
  local copies, waits for them, and re-layouts: 15.9 us -> 9.9 us
  other arithmetic: 3.26 us -> 0 us
    pallas_call x6 -> x1, Pallas kernels: 27.9 us -> 231 us  [fused(): pl.pallas_call(functools.partial(fused_kernel, spread), in_specs=[pl.Bloc...]
    all_to_all x4 -> x0, waiting for transfers between devices: 118 us -> none  [body(): sent = [lax.all_to_all(s, 'grid', 0, 0, tiled=True) for s in sent]]
    ppermute x2 -> x0, waiting for transfers between devices: 49.8 us -> none  [the longest x1 47 us: body(): lax.ppermute(visitors[-1], 'band', [(i, (i + span) % groups) for i in ran...]
    all_to_all x4 -> x0, starting transfers between devices: 23.8 us -> none  [body(): sent = [lax.all_to_all(s, 'grid', 0, 0, tiled=True) for s in sent]]
    unnamed x36 -> x18, local copies, waits for them, and re-layouts: 15.9 us -> 9.85 us
    ppermute x2 -> x0, starting transfers between devices: 3.57 us -> none  [the longest x1 3.07 us: body(): arrived = lax.ppermute(near, 'band', moves)]
    select_n x1 -> x0, other arithmetic: 3.26 us -> none  [body(): near = jnp.where((place >= reach) & (place < 2 * reach), arrived, near)]
  transfers between devices with their start and end apart: 6 -> 0, of which waited for: 5 -> 0; matrix products, arithmetic and copies ran while one was open for 0% -> 0% of each run, Pallas kernels for 7% -> 0%
where the time goes in v1:
time: 241 us
  Pallas kernels  231 us (96%)
  local copies, waits for them, and re-layouts  9.9 us (4%)
    pallas_call x1, Pallas kernels, fused(): pl.pallas_call(functools.partial(fused_kernel, spread), in_specs=[pl.Bloc...  231 us
    unnamed x18, local copies, waits for them, and re-layouts  9.85 us

profile of v1, /device:TPU:28, one launch (start us, length us, event | category | flops | bytes accessed | tf_op | source)
XLA Modules:
  0.0 240.7 jit_solution(8129292190337781040)
XLA Ops:
  0.0 0.0 copy-start
  0.0 1.2 copy-done
  1.3 0.0 copy-start.1
  1.3 1.6 copy-done.1
  2.9 0.0 copy-start.2
  2.9 0.9 copy-done.2
  3.9 0.0 copy-start.3
  3.9 0.9 copy-done.3
  4.8 0.0 copy-start.4
  4.8 0.9 copy-done.4
  5.8 0.0 copy-start.5
  5.8 0.9 copy-done.5
  6.7 0.0 copy-start.6
  6.7 0.9 copy-done.6
  7.7 0.0 copy-start.7
  7.7 0.9 copy-done.7
  8.6 230.8 %exchange_by_planes.1 = f32[1,2,16,128,128]{4,3,2,1,0:T(8,128)S(1)} custom-call(f32[1,2,16,128,128]{4,3,2,1,0:T(8,128)S(1)} %copy-done.1, f32[4,128,128]{2,1,0:T(8,128)S(1)} %bitcast.3, bf16[2,256,256]{2,1,0:T(8,128)(2,1)S(1)} %copy-done.7, bf16[2,256,256]{2,1,0:T(8,128)(2,1)S(1)} %copy-done.6, bf16[2,256,256]{2,1,0:T(8,128)(2,1)S(1)} %copy-done.5, ...), custom_call_target="tpu_custom_call" | custom-call | tf_op jit(solution)/shard_map/exchange_by_planes/pallas_call | solution.py:585
  239.4 1.3 copy.14
  (2 shorter events, 0.1 us)
Async XLA Ops:
  0.0 1.2 copy-start
  1.3 1.6 copy-start.1
  2.9 0.9 copy-start.2
  3.9 0.9 copy-start.3
  4.8 0.9 copy-start.4
  5.8 0.9 copy-start.5
  6.7 0.9 copy-start.6
  7.7 0.9 copy-start.7

commit v2 on v1

--- a/solution.py
+++ b/solution.py
@@ -229,13 +229,14 @@
 
 def fused_kernel(
     spread,
-    bands_ref, coulomb_ref, zf_ref, yf_ref, xf_ref, xi_ref, yi_ref, zi_ref,
+    bands_ref, coulomb_ref, tables_ref,
     out_ref,
-    held, screen, packed, lines, back, result, slab,
+    tabs, held, screen, packed, lines, back, result, slab,
     s1, r1, s2, r2, su, ru, sd, rd, s4, r4, s6, r6, s7, r7, s8, r8, loc,
 ):
     n = GROUPS
     peers = n * spread
+    zf_ref, yf_ref, xf_ref, xi_ref, yi_ref, zi_ref = (tabs.at[i] for i in range(6))
     band = lax.axis_index("band")
     grid = lax.axis_index("grid")
     z = grid // spread
@@ -281,11 +282,21 @@
         return pltpu.make_async_copy(chunk(h, band), held.at[h, z, slot], loc.at[h])
 
     screen_local = pltpu.make_async_copy(coulomb_ref, screen.at[z], loc.at[HALVES])
-    screen_local.start()
-    for h in range(HALVES):
-        first_local(h).start()
+    tables_local = pltpu.make_async_copy(tables_ref, tabs, loc.at[11])
+
+    def first_start(h):
         for d in (2, 1, 3):
             first(h, d).start()
+        first_local(h).start()
+
+    def first_wait(h):
+        first_local(h).wait()
+        for d in range(1, n):
+            first(h, d).wait_recv()
+
+    first_start(0)
+    screen_local.start()
+    tables_local.start()
 
     def block(stream, src):
         return held.at[stream, src, pl.ds(0, 2)] if stream < HALVES else screen.at[src]
@@ -341,21 +352,24 @@
         part = held.at[h, z, 2 + c]
         return remote(part, part, s2.at[h, c], r2.at[h, z], band, line(to))
 
-    for h in range(HALVES):
-        first_local(h).wait()
-        for d in range(1, n):
-            first(h, d).wait_recv()
-        hop(h, 0)
+    def direct_start(h):
         for c in range(2):
             @pl.when(z != c + 1)
             def _():
                 direct(h, c).start()
-        if h == 0:
-            hop(0, 1)
+
+    first_wait(0)
+    hop(0, 0)
+    first_start(1)
+    first_wait(1)
+    hop(0, 1)
+    direct_start(0)
+    hop(1, 0)
+    hop(0, 2)
+    direct_start(1)
+    hop(1, 1)
     screen_local.wait()
-    hop(1, 1)
-    hop(0, 2)
-    hop(HALVES, 0)
+    tables_local.wait()
 
     own = jnp.where(z == 0, 0, jnp.where(z == 1, 2, jnp.where(z == 2, 3, 1)))
 
@@ -370,12 +384,12 @@
                     device_id=(band, grid), device_id_type=pl.DeviceIdType.MESH,
                 ).wait_recv()
 
-    def fourth(h, k):
+    def fourth(h, v, k):
         q, to_band, to_grid = peer(k)
-        return remote(packed.at[h, q], lines.at[h, me], s4.at[h, k], r4.at[h, k], to_band, to_grid)
-
-    def fourth_local(h):
-        return pltpu.make_async_copy(packed.at[h, me], lines.at[h, me], loc.at[3 + h])
+        return remote(packed.at[h, q, v], lines.at[h, me, v], s4.at[h, v, k], r4.at[h, v, k], to_band, to_grid)
+
+    def fourth_local(h, v):
+        return pltpu.make_async_copy(packed.at[h, me, v], lines.at[h, me, v], loc.at[12 + 2 * h + v])
 
     def densities(h):
         @pl.loop(0, 2)
@@ -400,27 +414,47 @@
                         piece = done[part * ny:(part + 1) * ny, p * nz:(p + 1) * nz]
                         packed[h, :, v, :, part, i + p, :] = piece.reshape(peers, rows, nz)
 
-    for h in range(HALVES):
-        hop(h, 3)
-        received(h)
-        densities(h)
-        fourth_local(h).start()
+            for k in range(1, peers):
+                fourth(h, v, k).start()
+            fourth_local(h, v).start()
+
+    hop(0, 3)
+    received(0)
+    densities(0)
+    hop(1, 2)
+    hop(HALVES, 0)
+    hop(1, 3)
+    received(1)
+    densities(1)
+    for d in range(1, n):
+        hop(HALVES, d)
+
+    def sixth(h, v, k):
+        q, to_band, to_grid = peer(k)
+        return remote(packed.at[h, q, v], back.at[h, me, v], s6.at[h, v, k], r6.at[h, v, k], to_band, to_grid)
+
+    def sixth_local(h, v):
+        return pltpu.make_async_copy(packed.at[h, me, v], back.at[h, me, v], loc.at[16 + 2 * h + v])
+
+    def sixth_start(h, v):
         for k in range(1, peers):
-            fourth(h, k).start()
-        if h == 0:
-            hop(HALVES, 1)
-            hop(1, 2)
-            hop(HALVES, 2)
-    hop(HALVES, 3)
-
-    for h in range(HALVES):
-        fourth_local(h).wait()
+            sixth(h, v, k).start()
+        sixth_local(h, v).start()
+
+    def sixth_wait(h, v):
+        sixth_local(h, v).wait()
         for k in range(1, peers):
-            fourth(h, k).wait()
-
-    @pl.loop(0, n)
-    def _(src):
-        for v in range(2):
+            sixth(h, v, k).wait_recv()
+
+    @pl.loop(0, 2)
+    def _(v):
+        for h in range(HALVES):
+            fourth_local(h, v).wait()
+            for k in range(1, peers):
+                fourth(h, v, k).wait()
+
+        @pl.loop(0, n)
+        def _(src):
             for c in range(0, n, 2):
                 both = [
                     jnp.concatenate(
@@ -437,12 +471,7 @@
                         piece = value[part * nx:(part + 1) * nx, p * nz:(p + 1) * nz]
                         packed[:, :, v, src * n + c + p, part] = piece.reshape(HALVES, peers, 2 * n, nz)
 
-    def sixth(h, k):
-        q, to_band, to_grid = peer(k)
-        return remote(packed.at[h, q], back.at[h, me], s6.at[h, k], r6.at[h, k], to_band, to_grid)
-
-    def sixth_local(h):
-        return pltpu.make_async_copy(packed.at[h, me], back.at[h, me], loc.at[5 + h])
+        sixth_start(0, v)
 
     def seventh(h, to):
         return remote(result.at[h, to], slab.at[h, z], s7.at[h, to], r7.at[h, z], band, line(to))
@@ -458,11 +487,6 @@
 
     def eighth_local(h, src):
         return pltpu.make_async_copy(slab.at[h, src], out_part(band, h), loc.at[9 + h])
-
-    for h in range(HALVES):
-        sixth_local(h).start()
-        for k in range(1, peers):
-            sixth(h, k).start()
 
     def deliver(h):
         for src in range(n):
@@ -487,9 +511,10 @@
                 eighth(h, src).start()
 
     for h in range(HALVES):
-        sixth_local(h).wait()
-        for k in range(1, peers):
-            sixth(h, k).wait_recv()
+        for v in range(2):
+            sixth_wait(h, v)
+            if h == 0:
+                sixth_start(1, v)
         for src in range(n):
             for p in range(2):
                 i = src * 2 + p
@@ -532,8 +557,9 @@
             @pl.when(z != c + 1)
             def _():
                 direct(h, c).wait_send()
-        for k in range(1, peers):
-            sixth(h, k).wait_send()
+        for v in range(2):
+            for k in range(1, peers):
+                sixth(h, v, k).wait_send()
         for src in range(n):
             @pl.when(z != src)
             def _():
@@ -577,17 +603,18 @@
         + np.arange(HALVES)[:, None, None, None] * 2
         + np.arange(2)
     ).reshape(-1)
-    tabs = [jnp.asarray(t) for t in permuted_tables(nx, 1.0 / (nx * ny * nz), row_order, plane_order)]
+    tabs = jnp.asarray(np.stack(permuted_tables(nx, 1.0 / (nx * ny * nz), row_order, plane_order)))
     mine = lax.dynamic_slice_in_dim(coulomb, lax.axis_index("band") * n, n, axis=1).transpose(1, 0, 2)
     f32 = jnp.float32
     blocks = (HALVES, peers, 2, rows, 2, 2 * n, nz)
     sem = pltpu.SemaphoreType.DMA
     return pl.pallas_call(
         functools.partial(fused_kernel, spread),
-        in_specs=[pl.BlockSpec(memory_space=pl.ANY)] * 2 + [pl.BlockSpec(memory_space=pltpu.VMEM)] * 6,
+        in_specs=[pl.BlockSpec(memory_space=pl.ANY)] * 3,
         out_specs=pl.BlockSpec(memory_space=pl.ANY),
         out_shape=jax.ShapeDtypeStruct(bands.shape, f32),
         scratch_shapes=[
+            pltpu.VMEM(tabs.shape, tabs.dtype),
             pltpu.VMEM((HALVES, n, n, 2, 2, ny, nz), f32),
             pltpu.VMEM((n, n, nx, nz), f32),
             pltpu.VMEM(blocks, f32),
@@ -599,17 +626,17 @@
             sem((HALVES, 2)), sem((HALVES, n)),
             sem((HALVES + 1, n)), sem((HALVES + 1, n)),
             sem((HALVES + 1, n)), sem((HALVES + 1, n)),
-            sem((HALVES, peers)), sem((HALVES, peers)),
-            sem((HALVES, peers)), sem((HALVES, peers)),
+            sem((HALVES, 2, peers)), sem((HALVES, 2, peers)),
+            sem((HALVES, 2, peers)), sem((HALVES, 2, peers)),
             sem((HALVES, n)), sem((HALVES, n)),
             sem((HALVES, n)), sem((HALVES, n)),
-            sem((11,)),
+            sem((20,)),
         ],
         compiler_params=pltpu.CompilerParams(
-            collective_id=0, has_side_effects=True, vmem_limit_bytes=VMEM_LIMIT
+            collective_id=0, has_side_effects=True, vmem_limit_bytes=58 * 1024 * 1024
         ),
         name="exchange_by_planes",
-    )(bands, mine, *tabs)
+    )(bands, mine, tabs)
 
 
 def fits(bands, coulomb):

time: 241 us -> 214 us (0.89)
  Pallas kernels: 231 us -> 208 us
  local copies, waits for them, and re-layouts: 9.9 us -> 5.13 us
    pallas_call x1, Pallas kernels: 231 us -> 208 us  [fused(): pl.pallas_call(functools.partial(fused_kernel, spread), in_specs=[pl.Bloc...]
    unnamed x18 -> x4, local copies, waits for them, and re-layouts: 9.85 us -> 5.08 us
where the time goes in v2:
time: 214 us
  Pallas kernels  208 us (97%)
  local copies, waits for them, and re-layouts  5.13 us (2%)
    pallas_call x1, Pallas kernels, fused(): pl.pallas_call(functools.partial(fused_kernel, spread), in_specs=[pl.Bloc...  208 us
    unnamed x4, local copies, waits for them, and re-layouts  5.08 us

profile of v2, /device:TPU:28, one launch (start us, length us, event | category | flops | bytes accessed | tf_op | source)
XLA Modules:
  0.0 213.6 jit_solution(1580243654587553701)
XLA Ops:
  0.0 0.0 copy-start
  0.0 1.2 copy-done
  1.3 0.7 copy.7
  2.0 208.5 %exchange_by_planes.1 = f32[1,2,16,128,128]{4,3,2,1,0:T(8,128)} custom-call(f32[1,2,16,128,128]{4,3,2,1,0:T(8,128)} %bands_ref.1, f32[4,128,128]{2,1,0:T(8,128)} %bitcast.3, bf16[6,2,256,256]{3,2,1,0:T(8,128)(2,1)} %constant.13.clone.tables_ref), custom_call_target="tpu_custom_call" | custom-call | tf_op jit(solution)/shard_map/exchange_by_planes/pallas_call | solution.py:611
  210.5 3.1 %copy.9 = f32[1,2,16,128,128]{4,3,2,1,0:T(8,128)} copy(f32[1,2,16,128,128]{4,3,2,1,0:T(8,128)} %exchange_by_planes.1) | data formatting | bytes 4194304
  (1 shorter events, 0.0 us)
Async XLA Ops:
  0.0 1.2 copy-start

commit v3 on v2

--- a/solution.py
+++ b/solution.py
@@ -337,8 +337,8 @@
             def _():
                 down(stream, d).start()
 
-    def hops_sent(stream):
-        for d in range(n - 1):
+    def hops_sent(stream, distances):
+        for d in distances:
             @pl.when((z >= d) & (z + 1 < n))
             def _():
                 up(stream, d).wait_send()
@@ -358,16 +358,22 @@
             def _():
                 direct(h, c).start()
 
+    def direct_sent(h):
+        for c in range(2):
+            @pl.when(z != c + 1)
+            def _():
+                direct(h, c).wait_send()
+
     first_wait(0)
     hop(0, 0)
     first_start(1)
+    hop(0, 1)
+    hop(0, 2)
+    direct_start(0)
     first_wait(1)
-    hop(0, 1)
-    direct_start(0)
+    hops_sent(0, (0, 1, 2))
+    direct_sent(0)
     hop(1, 0)
-    hop(0, 2)
-    direct_start(1)
-    hop(1, 1)
     screen_local.wait()
     tables_local.wait()
 
@@ -421,7 +427,11 @@
     hop(0, 3)
     received(0)
     densities(0)
+    hop(1, 1)
     hop(1, 2)
+    direct_start(1)
+    hops_sent(1, (0, 1, 2))
+    direct_sent(1)
     hop(HALVES, 0)
     hop(1, 3)
     received(1)
@@ -513,7 +523,8 @@
     for h in range(HALVES):
         for v in range(2):
             sixth_wait(h, v)
-            if h == 0:
+        if h == 0:
+            for v in range(2):
                 sixth_start(1, v)
         for src in range(n):
             for p in range(2):
@@ -553,10 +564,6 @@
     for h in range(HALVES):
         for d in range(1, n):
             first(h, d).wait_send()
-        for c in range(2):
-            @pl.when(z != c + 1)
-            def _():
-                direct(h, c).wait_send()
         for v in range(2):
             for k in range(1, peers):
                 sixth(h, v, k).wait_send()
@@ -580,8 +587,7 @@
                     send_sem=s8.at[h, src], recv_sem=r8.at[h, src],
                     device_id=(band, grid), device_id_type=pl.DeviceIdType.MESH,
                 ).wait_recv()
-    for stream in range(HALVES + 1):
-        hops_sent(stream)
+    hops_sent(HALVES, (0, 1, 2))
 
 
 def fused(bands, coulomb):
@@ -633,7 +639,7 @@
             sem((20,)),
         ],
         compiler_params=pltpu.CompilerParams(
-            collective_id=0, has_side_effects=True, vmem_limit_bytes=58 * 1024 * 1024
+            collective_id=0, has_side_effects=True, vmem_limit_bytes=VMEM_LIMIT
         ),
         name="exchange_by_planes",
     )(bands, mine, tabs)

time: 214 us -> 210 us (0.981)
  Pallas kernels: 208 us -> 204 us
    pallas_call x1, Pallas kernels: 208 us -> 204 us  [fused(): pl.pallas_call(functools.partial(fused_kernel, spread), in_specs=[pl.Bloc...]
    unnamed x4 -> x8, local copies, waits for them, and re-layouts: 5.08 us -> 5.56 us
where the time goes in v3:
time: 210 us
  Pallas kernels  204 us (97%)
  local copies, waits for them, and re-layouts  5.61 us (3%)
    pallas_call x1, Pallas kernels, fused(): pl.pallas_call(functools.partial(fused_kernel, spread), in_specs=[pl.Bloc...  204 us
    unnamed x8, local copies, waits for them, and re-layouts  5.56 us

profile of v3, /device:TPU:28, one launch (start us, length us, event | category | flops | bytes accessed | tf_op | source)
XLA Modules:
  0.0 209.6 jit_solution(9484264335847743996)
XLA Ops:
  0.0 0.0 copy-start
  0.0 1.2 copy-done
  1.3 0.0 copy-start.1
  1.3 1.6 copy-done.1
  2.9 0.0 copy-start.2
  2.9 1.4 copy-done.2
  4.3 203.9 %exchange_by_planes.1 = f32[1,2,16,128,128]{4,3,2,1,0:T(8,128)S(1)} custom-call(f32[1,2,16,128,128]{4,3,2,1,0:T(8,128)S(1)} %copy-done.1, f32[4,128,128]{2,1,0:T(8,128)S(1)} %bitcast.3, bf16[6,2,256,256]{3,2,1,0:T(8,128)(2,1)S(1)} %copy-done.2), custom_call_target="tpu_custom_call" | custom-call | tf_op jit(solution)/shard_map/exchange_by_planes/pallas_call | solution.py:617
  208.3 1.3 copy.9
  (2 shorter events, 0.1 us)
Async XLA Ops:
  0.0 1.2 copy-start
  1.3 1.6 copy-start.1
  2.9 1.4 copy-start.2

commit v4 on v2

--- a/solution.py
+++ b/solution.py
@@ -222,7 +222,8 @@
 
 
 GROUPS = 4
-HALVES = 2
+ROUNDS = 4
+PLANES = GROUPS // ROUNDS
 PLANE_BAND = (0, 1, 3, 2)
 PLANE_SLOT = (0, 2, 3, 1)
 
@@ -244,7 +245,7 @@
     me = band * spread + t
     ny, nz = bands_ref.shape[3], bands_ref.shape[4]
     rows = ny // peers
-    nx = peers * 2 * n * HALVES
+    nx = peers * n * PLANES * ROUNDS
 
     def remote(src, dst, send, recv, to_band, to_grid):
         return pltpu.make_async_remote_copy(
@@ -272,17 +273,17 @@
     slot = (band % 2) * 2 + band // 2
 
     def chunk(h, j):
-        return bands_ref.at[0, :, pl.ds(j * n + h * 2, 2)]
+        return bands_ref.at[0, :, pl.ds(j * n + h * PLANES, PLANES)]
 
     def first(h, d):
         to = (band + d) % n
         return remote(chunk(h, to), held.at[h, z, slot], s1.at[h, d], r1.at[h, d], to, grid)
 
     def first_local(h):
-        return pltpu.make_async_copy(chunk(h, band), held.at[h, z, slot], loc.at[h])
-
-    screen_local = pltpu.make_async_copy(coulomb_ref, screen.at[z], loc.at[HALVES])
-    tables_local = pltpu.make_async_copy(tables_ref, tabs, loc.at[11])
+        return pltpu.make_async_copy(chunk(h, band), held.at[h, z, slot], loc.at[0, h])
+
+    screen_local = pltpu.make_async_copy(coulomb_ref, screen.at[z], loc.at[1, 0])
+    tables_local = pltpu.make_async_copy(tables_ref, tabs, loc.at[1, 1])
 
     def first_start(h):
         for d in (2, 1, 3):
@@ -299,7 +300,7 @@
     tables_local.start()
 
     def block(stream, src):
-        return held.at[stream, src, pl.ds(0, 2)] if stream < HALVES else screen.at[src]
+        return held.at[stream, src, pl.ds(0, 2)] if stream < ROUNDS else screen.at[src]
 
     def up(stream, d):
         return remote(
@@ -337,8 +338,8 @@
             def _():
                 down(stream, d).start()
 
-    def hops_sent(stream):
-        for d in range(n - 1):
+    def hops_sent(stream, distances):
+        for d in distances:
             @pl.when((z >= d) & (z + 1 < n))
             def _():
                 up(stream, d).wait_send()
@@ -357,19 +358,6 @@
             @pl.when(z != c + 1)
             def _():
                 direct(h, c).start()
-
-    first_wait(0)
-    hop(0, 0)
-    first_start(1)
-    first_wait(1)
-    hop(0, 1)
-    direct_start(0)
-    hop(1, 0)
-    hop(0, 2)
-    direct_start(1)
-    hop(1, 1)
-    screen_local.wait()
-    tables_local.wait()
 
     own = jnp.where(z == 0, 0, jnp.where(z == 1, 2, jnp.where(z == 2, 3, 1)))
 
@@ -389,21 +377,21 @@
         return remote(packed.at[h, q, v], lines.at[h, me, v], s4.at[h, v, k], r4.at[h, v, k], to_band, to_grid)
 
     def fourth_local(h, v):
-        return pltpu.make_async_copy(packed.at[h, me, v], lines.at[h, me, v], loc.at[12 + 2 * h + v])
+        return pltpu.make_async_copy(packed.at[h, me, v], lines.at[h, me, v], loc.at[2 + v, h])
 
     def densities(h):
         @pl.loop(0, 2)
         def _(v):
             reals, imags = [], []
             for src in range(n):
-                for p in range(2):
+                for p in range(PLANES):
                     own_re, own_im = held[h, src, own, 0, p], held[h, src, own, 1, p]
                     vis_re, vis_im = held[h, src, v, 0, p], held[h, src, v, 1, p]
                     reals.append(vis_re * own_re + vis_im * own_im)
                     imags.append(vis_re * own_im - vis_im * own_re)
             pair = jnp.concatenate([jnp.concatenate(reals, axis=0), jnp.concatenate(imags, axis=0)], axis=1)
             value = right(pair, zf_ref)
-            for i in range(0, 2 * n, 2):
+            for i in range(0, PLANES * n, 2):
                 both = [
                     jnp.concatenate([value[p * ny:(p + 1) * ny, :nz], value[p * ny:(p + 1) * ny, nz:]], axis=0)
                     for p in (i, i + 1)
@@ -418,23 +406,40 @@
                 fourth(h, v, k).start()
             fourth_local(h, v).start()
 
-    hop(0, 3)
-    received(0)
-    densities(0)
-    hop(1, 2)
-    hop(HALVES, 0)
-    hop(1, 3)
-    received(1)
-    densities(1)
-    for d in range(1, n):
-        hop(HALVES, d)
+    first_wait(0)
+    hop(0, 0)
+    first_start(1)
+    hop(0, 1)
+    screen_local.wait()
+    tables_local.wait()
+    for h in range(1, ROUNDS):
+        first_wait(h)
+        hop(h, 0)
+        if h + 1 < ROUNDS:
+            first_start(h + 1)
+        hop(h - 1, 2)
+        direct_start(h - 1)
+        hop(h, 1)
+        hop(h - 1, 3)
+        received(h - 1)
+        densities(h - 1)
+    last = ROUNDS - 1
+    hop(last, 2)
+    direct_start(last)
+    hop(ROUNDS, 0)
+    hop(last, 3)
+    received(last)
+    hop(ROUNDS, 1)
+    densities(last)
+    for d in range(2, n):
+        hop(ROUNDS, d)
 
     def sixth(h, v, k):
         q, to_band, to_grid = peer(k)
         return remote(packed.at[h, q, v], back.at[h, me, v], s6.at[h, v, k], r6.at[h, v, k], to_band, to_grid)
 
     def sixth_local(h, v):
-        return pltpu.make_async_copy(packed.at[h, me, v], back.at[h, me, v], loc.at[16 + 2 * h + v])
+        return pltpu.make_async_copy(packed.at[h, me, v], back.at[h, me, v], loc.at[4 + v, h])
 
     def sixth_start(h, v):
         for k in range(1, peers):
@@ -448,7 +453,7 @@
 
     @pl.loop(0, 2)
     def _(v):
-        for h in range(HALVES):
+        for h in range(ROUNDS):
             fourth_local(h, v).wait()
             for k in range(1, peers):
                 fourth(h, v, k).wait()
@@ -469,7 +474,7 @@
                 for p in range(2):
                     for part in range(2):
                         piece = value[part * nx:(part + 1) * nx, p * nz:(p + 1) * nz]
-                        packed[:, :, v, src * n + c + p, part] = piece.reshape(HALVES, peers, 2 * n, nz)
+                        packed[:, :, v, src * n + c + p, part] = piece.reshape(ROUNDS, peers, n * PLANES, nz)
 
         sixth_start(0, v)
 
@@ -477,16 +482,16 @@
         return remote(result.at[h, to], slab.at[h, z], s7.at[h, to], r7.at[h, z], band, line(to))
 
     def seventh_local(h, to):
-        return pltpu.make_async_copy(result.at[h, to], slab.at[h, to], loc.at[7 + h])
+        return pltpu.make_async_copy(result.at[h, to], slab.at[h, to], loc.at[6, h])
 
     def out_part(j, h):
-        return out_ref.at[0, :, pl.ds(j * n + h * 2, 2)]
+        return out_ref.at[0, :, pl.ds(j * n + h * PLANES, PLANES)]
 
     def eighth(h, src):
         return remote(slab.at[h, src], out_part(band, h), s8.at[h, src], r8.at[h, band], PLANE_BAND[src], grid)
 
     def eighth_local(h, src):
-        return pltpu.make_async_copy(slab.at[h, src], out_part(band, h), loc.at[9 + h])
+        return pltpu.make_async_copy(slab.at[h, src], out_part(band, h), loc.at[7, h])
 
     def deliver(h):
         for src in range(n):
@@ -510,14 +515,14 @@
             def _():
                 eighth(h, src).start()
 
-    for h in range(HALVES):
+    for h in range(ROUNDS):
         for v in range(2):
             sixth_wait(h, v)
-            if h == 0:
-                sixth_start(1, v)
+            if h + 1 < ROUNDS:
+                sixth_start(h + 1, v)
         for src in range(n):
-            for p in range(2):
-                i = src * 2 + p
+            for p in range(PLANES):
+                i = src * PLANES + p
                 both = [
                     jnp.concatenate([back[h, :, v, :, part, i, :].reshape(ny, nz) for part in range(2)], axis=0)
                     for v in range(2)
@@ -547,10 +552,11 @@
             @pl.when(z != src)
             def _():
                 seventh(h, src).start()
-    for h in range(HALVES):
-        deliver(h)
-
-    for h in range(HALVES):
+        if h > 0:
+            deliver(h - 1)
+    deliver(last)
+
+    for h in range(ROUNDS):
         for d in range(1, n):
             first(h, d).wait_send()
         for c in range(2):
@@ -580,8 +586,8 @@
                     send_sem=s8.at[h, src], recv_sem=r8.at[h, src],
                     device_id=(band, grid), device_id_type=pl.DeviceIdType.MESH,
                 ).wait_recv()
-    for stream in range(HALVES + 1):
-        hops_sent(stream)
+    for stream in range(ROUNDS + 1):
+        hops_sent(stream, (0, 1, 2))
 
 
 def fused(bands, coulomb):
@@ -600,13 +606,13 @@
         np.arange(n)[None, None, :, None] * (nx // n)
         + (q % spread)[None, :, None, None] * (nx // n // spread)
         + (q // spread)[None, :, None, None] * n
-        + np.arange(HALVES)[:, None, None, None] * 2
-        + np.arange(2)
+        + np.arange(ROUNDS)[:, None, None, None] * PLANES
+        + np.arange(PLANES)
     ).reshape(-1)
     tabs = jnp.asarray(np.stack(permuted_tables(nx, 1.0 / (nx * ny * nz), row_order, plane_order)))
     mine = lax.dynamic_slice_in_dim(coulomb, lax.axis_index("band") * n, n, axis=1).transpose(1, 0, 2)
     f32 = jnp.float32
-    blocks = (HALVES, peers, 2, rows, 2, 2 * n, nz)
+    blocks = (ROUNDS, peers, 2, rows, 2, n * PLANES, nz)
     sem = pltpu.SemaphoreType.DMA
     return pl.pallas_call(
         functools.partial(fused_kernel, spread),
@@ -615,25 +621,25 @@
         out_shape=jax.ShapeDtypeStruct(bands.shape, f32),
         scratch_shapes=[
             pltpu.VMEM(tabs.shape, tabs.dtype),
-            pltpu.VMEM((HALVES, n, n, 2, 2, ny, nz), f32),
+            pltpu.VMEM((ROUNDS, n, n, 2, PLANES, ny, nz), f32),
             pltpu.VMEM((n, n, nx, nz), f32),
             pltpu.VMEM(blocks, f32),
             pltpu.VMEM(blocks, f32),
             pltpu.VMEM(blocks, f32),
-            pltpu.VMEM((HALVES, n, 2, 2, ny, nz), f32),
-            pltpu.VMEM((HALVES, n, 2, 2, ny, nz), f32),
-            sem((HALVES, n)), sem((HALVES, n)),
-            sem((HALVES, 2)), sem((HALVES, n)),
-            sem((HALVES + 1, n)), sem((HALVES + 1, n)),
-            sem((HALVES + 1, n)), sem((HALVES + 1, n)),
-            sem((HALVES, 2, peers)), sem((HALVES, 2, peers)),
-            sem((HALVES, 2, peers)), sem((HALVES, 2, peers)),
-            sem((HALVES, n)), sem((HALVES, n)),
-            sem((HALVES, n)), sem((HALVES, n)),
-            sem((20,)),
+            pltpu.VMEM((ROUNDS, n, 2, PLANES, ny, nz), f32),
+            pltpu.VMEM((ROUNDS, n, 2, PLANES, ny, nz), f32),
+            sem((ROUNDS, n)), sem((ROUNDS, n)),
+            sem((ROUNDS, 2)), sem((ROUNDS, n)),
+            sem((ROUNDS + 1, n)), sem((ROUNDS + 1, n)),
+            sem((ROUNDS + 1, n)), sem((ROUNDS + 1, n)),
+            sem((ROUNDS, 2, peers)), sem((ROUNDS, 2, peers)),
+            sem((ROUNDS, 2, peers)), sem((ROUNDS, 2, peers)),
+            sem((ROUNDS, n)), sem((ROUNDS, n)),
+            sem((ROUNDS, n)), sem((ROUNDS, n)),
+            sem((8, ROUNDS)),
         ],
         compiler_params=pltpu.CompilerParams(
-            collective_id=0, has_side_effects=True, vmem_limit_bytes=58 * 1024 * 1024
+            collective_id=0, has_side_effects=True, vmem_limit_bytes=VMEM_LIMIT
         ),
         name="exchange_by_planes",
     )(bands, mine, tabs)
@@ -645,7 +651,7 @@
         bands.shape[0] == 1
         and groups == GROUPS
         and shards % GROUPS == 0
-        and bands.shape[2] == 2 * HALVES * GROUPS
+        and bands.shape[2] == GROUPS * GROUPS
         and bands.shape[3] == GROUPS * GROUPS * shards
         and coulomb.shape[0] == bands.shape[3] == bands.shape[4]
     )

time: 214 us -> 186 us (0.87)
  Pallas kernels: 208 us -> 180 us
    pallas_call x1, Pallas kernels: 208 us -> 180 us  [fused(): pl.pallas_call(functools.partial(fused_kernel, spread), in_specs=[pl.Bloc...]
    unnamed x4 -> x8, local copies, waits for them, and re-layouts: 5.08 us -> 5.56 us
where the time goes in v4:
time: 186 us; the launch traced here: 185 us
  Pallas kernels  180 us (97%)
  local copies, waits for them, and re-layouts  5.61 us (3%)
    pallas_call x1, Pallas kernels, fused(): pl.pallas_call(functools.partial(fused_kernel, spread), in_specs=[pl.Bloc...  180 us
    unnamed x8, local copies, waits for them, and re-layouts  5.56 us

profile of v4, /device:TPU:28, one launch (start us, length us, event | category | flops | bytes accessed | tf_op | source)
XLA Modules:
  0.0 185.4 jit_solution(17610515773340727944)
XLA Ops:
  0.0 0.0 copy-start
  0.0 1.2 copy-done
  1.3 0.0 copy-start.1
  1.3 1.6 copy-done.1
  2.9 0.0 copy-start.2
  2.9 1.4 copy-done.2
  4.3 179.8 %exchange_by_planes.1 = f32[1,2,16,128,128]{4,3,2,1,0:T(8,128)S(1)} custom-call(f32[1,2,16,128,128]{4,3,2,1,0:T(8,128)S(1)} %copy-done.1, f32[4,128,128]{2,1,0:T(8,128)S(1)} %bitcast.3, bf16[6,2,256,256]{3,2,1,0:T(8,128)(2,1)S(1)} %copy-done.2), custom_call_target="tpu_custom_call" | custom-call | tf_op jit(solution)/shard_map/exchange_by_planes/pallas_call | solution.py:617
  184.1 1.3 copy.9
  (2 shorter events, 0.1 us)
Async XLA Ops:
  0.0 1.2 copy-start
  1.3 1.6 copy-start.1
  2.9 1.4 copy-start.2

commit v5 on v4

--- a/solution.py
+++ b/solution.py
@@ -209,15 +209,12 @@
     rows = np.concatenate([row_order, row_order + length])
     planes = np.concatenate([plane_order, plane_order + length])
     return [
-        split_table(t)
-        for t in (
-            forward.T,
-            forward[rows],
-            forward[:, planes],
-            inverse[planes] * scale,
-            inverse[:, rows],
-            inverse.T,
-        )
+        forward.T,
+        forward[rows],
+        forward[:, planes],
+        inverse[planes] * scale,
+        inverse[:, rows],
+        inverse.T,
     ]
 
 
@@ -232,7 +229,7 @@
     spread,
     bands_ref, coulomb_ref, tables_ref,
     out_ref,
-    tabs, held, screen, packed, lines, back, result, slab,
+    whole_tabs, tabs, weights, held, screen, packed, lines, back, result, slab,
     s1, r1, s2, r2, su, ru, sd, rd, s4, r4, s6, r6, s7, r7, s8, r8, loc,
 ):
     n = GROUPS
@@ -282,8 +279,9 @@
     def first_local(h):
         return pltpu.make_async_copy(chunk(h, band), held.at[h, z, slot], loc.at[0, h])
 
-    screen_local = pltpu.make_async_copy(coulomb_ref, screen.at[z], loc.at[1, 0])
-    tables_local = pltpu.make_async_copy(tables_ref, tabs, loc.at[1, 1])
+    tile = pl.multiple_of((band // 2) * 2 * n, 2 * n)
+    weights_local = pltpu.make_async_copy(coulomb_ref.at[:, pl.ds(tile, 2 * n)], weights, loc.at[1, 0])
+    tables_local = pltpu.make_async_copy(tables_ref, whole_tabs, loc.at[1, 1])
 
     def first_start(h):
         for d in (2, 1, 3):
@@ -296,7 +294,7 @@
             first(h, d).wait_recv()
 
     first_start(0)
-    screen_local.start()
+    weights_local.start()
     tables_local.start()
 
     def block(stream, src):
@@ -406,12 +404,17 @@
                 fourth(h, v, k).start()
             fourth_local(h, v).start()
 
+    weights_local.wait()
+    for c in range(n):
+        screen[z, c] = jnp.where(band % 2 == 0, weights[:, c], weights[:, n + c])
+    hop(ROUNDS, 0)
     first_wait(0)
     hop(0, 0)
     first_start(1)
     hop(0, 1)
-    screen_local.wait()
     tables_local.wait()
+    for i in range(6):
+        tabs[i, 0], tabs[i, 1] = split(whole_tabs[i])
     for h in range(1, ROUNDS):
         first_wait(h)
         hop(h, 0)
@@ -426,10 +429,9 @@
     last = ROUNDS - 1
     hop(last, 2)
     direct_start(last)
-    hop(ROUNDS, 0)
+    hop(ROUNDS, 1)
     hop(last, 3)
     received(last)
-    hop(ROUNDS, 1)
     densities(last)
     for d in range(2, n):
         hop(ROUNDS, d)
@@ -609,18 +611,21 @@
         + np.arange(ROUNDS)[:, None, None, None] * PLANES
         + np.arange(PLANES)
     ).reshape(-1)
-    tabs = jnp.asarray(np.stack(permuted_tables(nx, 1.0 / (nx * ny * nz), row_order, plane_order)))
-    mine = lax.dynamic_slice_in_dim(coulomb, lax.axis_index("band") * n, n, axis=1).transpose(1, 0, 2)
+    tabs = jnp.asarray(
+        np.stack(permuted_tables(nx, 1.0 / (nx * ny * nz), row_order, plane_order)).astype(np.float32)
+    )
     f32 = jnp.float32
     blocks = (ROUNDS, peers, 2, rows, 2, n * PLANES, nz)
     sem = pltpu.SemaphoreType.DMA
     return pl.pallas_call(
         functools.partial(fused_kernel, spread),
-        in_specs=[pl.BlockSpec(memory_space=pl.ANY)] * 3,
+        in_specs=[pl.BlockSpec(memory_space=pltpu.HBM)] * 3,
         out_specs=pl.BlockSpec(memory_space=pl.ANY),
         out_shape=jax.ShapeDtypeStruct(bands.shape, f32),
         scratch_shapes=[
-            pltpu.VMEM(tabs.shape, tabs.dtype),
+            pltpu.VMEM(tabs.shape, f32),
+            pltpu.VMEM(tabs.shape[:1] + (2,) + tabs.shape[1:], jnp.bfloat16),
+            pltpu.VMEM((nx, 2 * n, nz), f32),
             pltpu.VMEM((ROUNDS, n, n, 2, PLANES, ny, nz), f32),
             pltpu.VMEM((n, n, nx, nz), f32),
             pltpu.VMEM(blocks, f32),
@@ -642,7 +647,7 @@
             collective_id=0, has_side_effects=True, vmem_limit_bytes=VMEM_LIMIT
         ),
         name="exchange_by_planes",
-    )(bands, mine, tabs)
+    )(bands, coulomb, tabs)
 
 
 def fits(bands, coulomb):

time: 186 us -> 179 us (0.962)
  Pallas kernels: 180 us -> 174 us
    pallas_call x1, Pallas kernels: 180 us -> 174 us  [fused(): pl.pallas_call(functools.partial(fused_kernel, spread), in_specs=[pl.Bloc...]
    unnamed x8 -> x5, local copies, waits for them, and re-layouts: 5.56 us -> 3.95 us
where the time goes in v5:
time: 179 us; the launch traced here: 178 us
  Pallas kernels  174 us (97%)
  local copies, waits for them, and re-layouts  3.95 us (2%)
    pallas_call x1, Pallas kernels, fused(): pl.pallas_call(functools.partial(fused_kernel, spread), in_specs=[pl.Bloc...  174 us
    unnamed x5, local copies, waits for them, and re-layouts  3.95 us

profile of v5, /device:TPU:28, one launch (start us, length us, event | category | flops | bytes accessed | tf_op | source)
XLA Modules:
  0.0 178.4 jit_solution(13869443058313701933)
XLA Ops:
  0.0 0.0 copy-start
  0.0 1.4 copy-done
  1.4 0.0 copy-start.1
  1.4 1.2 copy-done.1
  2.6 174.4 %exchange_by_planes.1 = f32[1,2,16,128,128]{4,3,2,1,0:T(8,128)S(1)} custom-call(f32[1,2,16,128,128]{4,3,2,1,0:T(8,128)} %bands_ref.1, f32[128,16,128]{2,1,0:T(8,128)S(1)} %copy-done.1, f32[6,256,256]{2,1,0:T(8,128)S(1)} %copy-done), custom_call_target="tpu_custom_call" | custom-call | tf_op jit(solution)/shard_map/exchange_by_planes/pallas_call | solution.py:620
  177.0 1.3 copy.5
Async XLA Ops:
  0.0 1.4 copy-start
  1.4 1.2 copy-start.1

commit v6 on v5

--- a/solution.py
+++ b/solution.py
@@ -423,13 +423,17 @@
         hop(h - 1, 2)
         direct_start(h - 1)
         hop(h, 1)
-        hop(h - 1, 3)
-        received(h - 1)
-        densities(h - 1)
+        if h > 1:
+            hop(h - 2, 3)
+            received(h - 2)
+            densities(h - 2)
     last = ROUNDS - 1
     hop(last, 2)
     direct_start(last)
     hop(ROUNDS, 1)
+    hop(last - 1, 3)
+    received(last - 1)
+    densities(last - 1)
     hop(last, 3)
     received(last)
     densities(last)
@@ -554,8 +558,9 @@
             @pl.when(z != src)
             def _():
                 seventh(h, src).start()
-        if h > 0:
-            deliver(h - 1)
+        if h > 1:
+            deliver(h - 2)
+    deliver(last - 1)
     deliver(last)
 
     for h in range(ROUNDS):

time: 179 us -> 182 us (1.017)
  Pallas kernels: 174 us -> 177 us
    pallas_call x1, Pallas kernels: 174 us -> 177 us  [fused(): pl.pallas_call(functools.partial(fused_kernel, spread), in_specs=[pl.Bloc...]
where the time goes in v6:
time: 182 us; the launch traced here: 181 us
  Pallas kernels  177 us (97%)
  local copies, waits for them, and re-layouts  3.95 us (2%)
    pallas_call x1, Pallas kernels, fused(): pl.pallas_call(functools.partial(fused_kernel, spread), in_specs=[pl.Bloc...  177 us
    unnamed x5, local copies, waits for them, and re-layouts  3.95 us

profile of v6, /device:TPU:28, one launch (start us, length us, event | category | flops | bytes accessed | tf_op | source)
XLA Modules:
  0.0 180.9 jit_solution(15829480632302654722)
XLA Ops:
  0.0 0.0 copy-start
  0.0 1.4 copy-done
  1.4 0.0 copy-start.1
  1.4 1.2 copy-done.1
  2.6 176.9 %exchange_by_planes.1 = f32[1,2,16,128,128]{4,3,2,1,0:T(8,128)S(1)} custom-call(f32[1,2,16,128,128]{4,3,2,1,0:T(8,128)} %bands_ref.1, f32[128,16,128]{2,1,0:T(8,128)S(1)} %copy-done.1, f32[6,256,256]{2,1,0:T(8,128)S(1)} %copy-done), custom_call_target="tpu_custom_call" | custom-call | tf_op jit(solution)/shard_map/exchange_by_planes/pallas_call | solution.py:625
  179.6 1.3 copy.5
Async XLA Ops:
  0.0 1.4 copy-start
  1.4 1.2 copy-start.1

commit v7 on v5

--- a/solution.py
+++ b/solution.py
@@ -554,8 +554,9 @@
             @pl.when(z != src)
             def _():
                 seventh(h, src).start()
-        if h > 0:
-            deliver(h - 1)
+        if h > 1:
+            deliver(h - 2)
+    deliver(last - 1)
     deliver(last)
 
     for h in range(ROUNDS):

time: 179 us -> 178 us (level); the launches traced: 178 us -> 175 us
  Pallas kernels: 174 us -> 171 us
    pallas_call x1, Pallas kernels: 174 us -> 171 us  [fused(): pl.pallas_call(functools.partial(fused_kernel, spread), in_specs=[pl.Bloc...]
where the time goes in v7:
time: 178 us; the launch traced here: 175 us
  Pallas kernels  171 us (96%)
  local copies, waits for them, and re-layouts  3.95 us (2%)
    pallas_call x1, Pallas kernels, fused(): pl.pallas_call(functools.partial(fused_kernel, spread), in_specs=[pl.Bloc...  171 us
    unnamed x5, local copies, waits for them, and re-layouts  3.95 us

profile of v7, /device:TPU:28, one launch (start us, length us, event | category | flops | bytes accessed | tf_op | source)
XLA Modules:
  0.0 175.1 jit_solution(9186207432407320759)
XLA Ops:
  0.0 0.0 copy-start
  0.0 1.4 copy-done
  1.4 0.0 copy-start.1
  1.4 1.2 copy-done.1
  2.6 171.1 %exchange_by_planes.1 = f32[1,2,16,128,128]{4,3,2,1,0:T(8,128)S(1)} custom-call(f32[1,2,16,128,128]{4,3,2,1,0:T(8,128)} %bands_ref.1, f32[128,16,128]{2,1,0:T(8,128)S(1)} %copy-done.1, f32[6,256,256]{2,1,0:T(8,128)S(1)} %copy-done), custom_call_target="tpu_custom_call" | custom-call | tf_op jit(solution)/shard_map/exchange_by_planes/pallas_call | solution.py:621
  173.8 1.3 copy.5
Async XLA Ops:
  0.0 1.4 copy-start
  1.4 1.2 copy-start.1
